TPU v7x, 32 devices: a whole 2x2x4 slice. The times are simulated.
32 devices in a mesh: row: 4 (over y, core), col: 8 (over z, x).
Axes of the slice: x: 2, y: 2, z: 4, core: 2. Of those that a mesh axis runs over, the one named last changes fastest.
Arguments:
- weight: bfloat16 [8192, 26624], P('row', 'col'), may hold values from -0.59765625 to 0.59765625
- momentum: bfloat16 [8192, 26624], P('row', 'col'), may hold values from -6 to 6
- grad: bfloat16 [8192, 26624], P('row', 'col'), may hold values from -52 to 52
- right_factor: float32 [26624, 512], P('col'), may hold values from -6 to 6
Outputs:
- weight_next: bfloat16 [8192, 26624], P('row', 'col')
- momentum_next: bfloat16 [8192, 26624], P('row', 'col')
- right_next: float32 [26624, 512], P('col')
All inputs are finite; a program needn't handle non-finite values.
Results may differ from a plain program's by a relative error of at most 0.009.
Values may be sent and summed in bfloat16 or wider, within the bound.
No kernel may reach another device: no remote copies, remote signals or barrier semaphores. Data moves between devices by JAX's collectives and lax.ppermute only.
A program may use at most 256 MiB of HBM per device.

v0:
```python
import jax
import jax.numpy as jnp
from jax import lax
from jax.sharding import PartitionSpec as P

FF = 26624


FEEDBACK_CUT = 0.25
STEP_SIZE = 0.1
EPSILON_SQ = 1e-06


def orthonormal(left_prod, gram_mat):
    factor_low = jnp.linalg.cholesky(gram_mat)
    return lax.linalg.triangular_solve(
        factor_low, left_prod, left_side=False, lower=True, transpose_a=True
    )


def gram_of(left_prod):
    return jnp.dot(
        left_prod.T, left_prod, precision=lax.Precision.HIGHEST, preferred_element_type=jnp.float32
    )


def on_device(weight, momentum, grad, right_factor):
    buffer = (momentum.astype(jnp.float32) + grad.astype(jnp.float32)).astype(jnp.bfloat16)
    right_in = right_factor.astype(jnp.bfloat16)
    left_prod = lax.psum(jnp.dot(buffer, right_in, preferred_element_type=jnp.float32), "col")
    gram_mat = lax.psum(gram_of(left_prod), "row")
    ortho_rows = orthonormal(left_prod, gram_mat).astype(jnp.bfloat16)
    back_part = jnp.einsum("ij,ik->jk", buffer, ortho_rows, preferred_element_type=jnp.float32)
    scale_top = jnp.sqrt(jnp.float32(FF))
    back_share = lax.psum_scatter(back_part, "row", scatter_dimension=0, tiled=True)
    squares = lax.psum(jnp.sum(back_share * back_share, axis=0), ("row", "col"))
    right_share = back_share * (scale_top / jnp.sqrt(squares + EPSILON_SQ))
    back_prod, right_next = (
        lax.all_gather(back_share, "row", axis=0, tiled=True),
        lax.all_gather(right_share, "row", axis=0, tiled=True),
    )
    back_half = back_prod.astype(jnp.bfloat16)
    right_half = right_next.astype(jnp.bfloat16)
    feedback = jnp.einsum("ik,jk->ij", ortho_rows, back_half, preferred_element_type=jnp.float32)
    momentum_next = (buffer.astype(jnp.float32) - FEEDBACK_CUT * feedback).astype(jnp.bfloat16)
    update = jnp.einsum("ik,jk->ij", ortho_rows, right_half, preferred_element_type=jnp.float32)
    weight_next = (weight.astype(jnp.float32) - STEP_SIZE * update).astype(jnp.bfloat16)
    return (weight_next, momentum_next, right_next)


def solution(mesh):
    in_specs = (P("row", "col"), P("row", "col"), P("row", "col"), P("col", None))
    out_specs = (P("row", "col"), P("row", "col"), P("col", None))
    return jax.shard_map(
        on_device, mesh=mesh, in_specs=in_specs, out_specs=out_specs, check_vma=False
    )
```

profile of v0, /device:TPU:0, one launch (start us, length us, event | category | flops | bytes accessed | tf_op | source)
XLA Modules:
  0.0 589.6 jit_solution(11819488099148084249)
XLA Ops:
  7.2 15.7 %fusion.2 = f32[2048,512]{1,0:T(8,128)} fusion(f32[3328,512]{1,0:T(8,128)} %param.7, bf16[2048,3328]{1,0:T(8,128)(2,1)} %param.6, bf16[2048,3328]{1,0:T(8,128)(2,1)} %param.5), kind=kOutput, calls=%fused_computation.7 | convolution fusion | flops 7008288768 | bytes 38273024 | tf_op jit(solution)/shard_map/dot_general | solution.py:30
  23.0 159.1 %all-reduce.4.cloned.1.call-done = f32[2048,512]{1,0:T(8,128)} async-done(((f32[2048,512]{1,0:T(8,128)}), f32[2048,512]{1,0:T(8,128)}) %all-reduce.4.cloned.1.call-update) | async-done | bytes 4194320 | tf_op jit(solution)/shard_map/psum | solution.py:30
  182.1 11.4 %fusion.42 = f32[512,512]{0,1:T(8,128)} fusion(f32[2048,512]{1,0:T(8,128)} %all-reduce.4.cloned.1.call-done), kind=kOutput, calls=%fused_computation.82 | convolution fusion | flops 6442450944 | bytes 5242880 | tf_op jit(solution)/shard_map/dot_general | solution.py:22
  193.8 35.0 %all-reduce.6.cloned.1.call-done = f32[512,512]{0,1:T(8,128)} async-done(((f32[512,512]{0,1:T(8,128)}), f32[512,512]{0,1:T(8,128)}) %all-reduce.6.cloned.1.call-update) | async-done | bytes 1048592 | tf_op jit(solution)/shard_map/psum | solution.py:31
  231.8 11.7 %cholesky.104 = f32[128,128]{1,0:T(8,128)S(1)} custom-call(f32[128,128]{1,0:T(8,128)S(1)} %cholesky.266), custom_call_target="Cholesky" | custom-call | tf_op jit(solution)/shard_map/jit(cholesky)/cholesky | solution.py:15
  243.6 9.8 %custom-call.30 = f32[1,128,128]{1,2,0:T(8,128)S(1)} custom-call(f32[1,128,128]{2,1,0:T(8,128)S(1)} %get-tuple-element.30), custom_call_target="InvertDiagBlocksLowerTriangular" | custom-call | tf_op jit(solution)/shard_map/jit(cholesky)/cholesky | solution.py:15
  254.2 11.7 %cholesky.217 = f32[128,128]{1,0:T(8,128)S(1)} custom-call(f32[128,128]{1,0:T(8,128)S(1)} %cholesky.270), custom_call_target="Cholesky" | custom-call | tf_op jit(solution)/shard_map/jit(cholesky)/cholesky | solution.py:15
  265.9 10.3 %custom-call.31 = f32[1,128,128]{1,2,0:T(8,128)S(1)} custom-call(f32[1,128,128]{2,1,0:T(8,128)S(1)} %get-tuple-element.27), custom_call_target="InvertDiagBlocksLowerTriangular" | custom-call | tf_op jit(solution)/shard_map/jit(cholesky)/cholesky | solution.py:15
  276.9 11.7 %cholesky.238 = f32[128,128]{1,0:T(8,128)S(1)} custom-call(f32[128,128]{1,0:T(8,128)S(1)} %cholesky.275), custom_call_target="Cholesky" | custom-call | tf_op jit(solution)/shard_map/jit(cholesky)/cholesky | solution.py:15
  289.3 9.8 %custom-call.32 = f32[1,128,128]{1,2,0:T(8,128)S(1)} custom-call(f32[1,128,128]{2,1,0:T(8,128)S(1)} %get-tuple-element.24), custom_call_target="InvertDiagBlocksLowerTriangular" | custom-call | tf_op jit(solution)/shard_map/jit(cholesky)/cholesky | solution.py:15
  299.7 11.7 %cholesky.255 = f32[128,128]{1,0:T(8,128)S(1)} custom-call(f32[128,128]{1,0:T(8,128)S(1)} %convolution_subtract_fusion.4), custom_call_target="Cholesky" | custom-call | tf_op jit(solution)/shard_map/jit(cholesky)/cholesky | solution.py:15
  315.6 8.0 %while.1 = (s32[]{:T(128)}, f32[512,512]{1,0:T(8,128)S(1)}, s32[4,2]{0,1:T(2,128)S(1)}, f32[4,128,128]{2,1,0:T(8,128)S(1)}, s32[]{:T(128)}) while((s32[]{:T(128)}, f32[512,512]{1,0:T(8,128)S(1)}, s32[4,2]{0,1:T(2,128)S(1)}, f32[4,128,128]{2,1,0:T(8,128)S(1)}, s32[]{:T(128)}) %tuple.34), condition=%wide.while_cond, body=%wide.while_body.sunk | while | flops 2 | bytes 131181 | solution.py:16
  323.6 39.3 %custom-call.33 = f32[4,128,128]{1,2,0:T(8,128)S(1)} custom-call(f32[4,128,128]{2,1,0:T(8,128)S(1)} %get-tuple-element.10), custom_call_target="InvertDiagBlocksLowerTriangular" | custom-call | tf_op jit(solution)/shard_map/triangular_solve | solution.py:16
  365.4 3.0 convolution_subtract_fusion.1
  369.6 3.6 convolution_subtract_fusion
  374.3 5.6 fusion.10
  381.0 14.3 %fusion.37 = f32[3328,512]{1,0:T(8,128)} fusion(bf16[2048,128]{0,1:T(8,128)(2,1)S(1)} %convolution_convert_fusion, bf16[2048,128]{0,1:T(8,128)(2,1)S(1)} %get-tuple-element.33, bf16[2048,128]{0,1:T(8,128)(2,1)S(1)} %get-tuple-element.35, bf16[2048,128]{0,1:T(8,128)(2,1)S(1)} %get-tuple-element.37, bf16[2048,3328]{1,0:T(8,128)(2,1)} %param.6, ...), kind=kOutput, calls=%fused_computation.77 | convolution fusion | flops 7014973440 | bytes 36175872 | tf_op jit(solution)/shard_map/ij,ik->jk/dot_general | solution.py:33
  395.4 62.3 %reduce-scatter.2.cloned.1.call-done = f32[832,512]{1,0:T(8,128)} async-done(((f32[3328,512]{1,0:T(8,128)}), f32[832,512]{1,0:T(8,128)}) %reduce-scatter.2.cloned.1.call-update) | async-done | bytes 1703952 | tf_op jit(solution)/shard_map/reduce_scatter | solution.py:35
  459.5 40.1 %psum.23 = f32[512]{0:T(512)S(1)} all-reduce(f32[512]{0:T(512)S(1)} %multiply_reduce_fusion), channel_id=1, replica_groups=mesh['row'=4,'col'=8] {'row','col'}, use_global_device_ids=true, to_apply=%region_12.13 | all-reduce | flops 512 | bytes 4096 | tf_op jit(solution)/shard_map/psum | solution.py:36
  501.0 8.4 %all-gather.5.cloned.1.call-done = f32[3328,512]{1,0:T(8,128)} async-done(((f32[832,512]{1,0:T(8,128)}), f32[3328,512]{1,0:T(8,128)}) %all-gather.5.cloned.1.call-update) | async-done | bytes 6815760 | tf_op jit(solution)/shard_map/all_gather | solution.py:39
  509.4 19.6 %subtract_convert_fusion = bf16[2048,3328]{1,0:T(8,128)(2,1)} fusion(f32[3328,512]{1,0:T(8,128)} %all-gather.5.cloned.1.call-done, bf16[2048,128]{0,1:T(8,128)(2,1)S(1)} %convolution_convert_fusion, bf16[2048,128]{0,1:T(8,128)(2,1)} %copy-done.2, bf16[2048,128]{0,1:T(8,128)(2,1)S(1)} %get-tuple-element.35, bf16[2048,128]{0,1:T(8,128)(2,1)S(1)} %get-tuple-element.37, ...), kind=kOutput, calls=%fused_computation.2 | convolution fusion | flops 7043940352 | bytes 49807360 | tf_op jit(solution)/shard_map/ik,jk->ij/dot_general | solution.py:44
  529.0 31.7 %all-gather.3.cloned.1.call-done = f32[3328,512]{1,0:T(8,128)} async-done(((f32[832,512]{1,0:T(8,128)}), f32[3328,512]{1,0:T(8,128)}) %all-gather.3.cloned.1.call-update) | async-done | bytes 6815760 | tf_op jit(solution)/shard_map/all_gather | solution.py:40
  560.8 15.3 %subtract_convert_fusion.1 = bf16[2048,3328]{1,0:T(8,128)(2,1)} fusion(bf16[2048,3328]{1,0:T(8,128)(2,1)} %param.4, f32[3328,512]{1,0:T(8,128)} %all-gather.3.cloned.1.call-done, bf16[2048,128]{0,1:T(8,128)(2,1)S(1)} %convolution_convert_fusion, bf16[2048,128]{0,1:T(8,128)(2,1)S(1)} %copy-done.3, bf16[2048,128]{0,1:T(8,128)(2,1)S(1)} %get-tuple-element.35, ...), kind=kOutput, calls=%fused_computation.3 | convolution fusion | flops 7016677376 | bytes 36175872 | tf_op jit(solution)/shard_map/ik,jk->ij/dot_general | solution.py:46
  576.1 6.6 %copy.28 = f32[3328,512]{1,0:T(8,128)} copy(f32[3328,512]{1,0:T(8,128)} %all-gather.3.cloned.1.call-done) | data formatting | bytes 13631488
  (60 shorter events, 24.7 us)
Async XLA Ops:
  7.2 175.0 %all-reduce.4.cloned.1.call-start = ((), (), s32[]{:S(2)}) async-start(), calls=%async_computation.1 | async-start | bytes 8388608 | tf_op jit(solution)/shard_map/psum | solution.py:30
  23.0 205.8 %all-reduce.6.cloned.1.call-start = ((), (), s32[]{:S(2)}) async-start(), calls=%async_computation.2 | async-start | bytes 2097152 | tf_op jit(solution)/shard_map/psum | solution.py:31
  193.5 264.1 %reduce-scatter.2.cloned.1.call-start = ((), (), s32[]{:S(2)}) async-start(), calls=%async_computation.3 | async-start | bytes 8519680 | tf_op jit(solution)/shard_map/reduce_scatter | solution.py:35
  362.9 6.6 %copy-start = (f32[2048,512]{1,0:T(8,128)S(1)}, f32[2048,512]{1,0:T(8,128)}, u32[]{:S(2)}) copy-start(f32[2048,512]{1,0:T(8,128)} %all-reduce.4.cloned.1.call-done) | copy-start | bytes 12582916
  374.3 6.7 %copy-start.2 = (bf16[2048,128]{0,1:T(8,128)(2,1)}, bf16[2048,128]{0,1:T(8,128)(2,1)S(1)}, u32[]{:S(2)}) copy-start(bf16[2048,128]{0,1:T(8,128)(2,1)S(1)} %get-tuple-element.33) | copy-start | bytes 1572868
  395.3 114.1 %all-gather.5.cloned.1.call-start = ((), (), s32[]{:S(2)}) async-start(), calls=%async_computation.5 | async-start | bytes 8519680 | tf_op jit(solution)/shard_map/all_gather | solution.py:39
  457.7 41.9 %copy-start.1 = (f32[832,512]{1,0:T(8,128)S(1)}, f32[832,512]{1,0:T(8,128)}, u32[]{:S(2)}) copy-start(f32[832,512]{1,0:T(8,128)} %reduce-scatter.2.cloned.1.call-done) | copy-start | bytes 5111812
  457.7 103.0 %all-gather.3.cloned.1.call-start = ((), (), s32[]{:S(2)}) async-start(), calls=%async_computation.4 | async-start | bytes 8519680 | tf_op jit(solution)/shard_map/all_gather | solution.py:40
  501.0 59.8 %copy-start.3 = (bf16[2048,128]{0,1:T(8,128)(2,1)S(1)}, bf16[2048,128]{0,1:T(8,128)(2,1)}, u32[]{:S(2)}) copy-start(bf16[2048,128]{0,1:T(8,128)(2,1)} %copy-done.2) | copy-start | bytes 1572868
Sparse Core Ops, SparseCore 0:
  23.1 158.9 all-reduce.3
  193.7 35.0 all-reduce.5
  395.4 62.2 reduce-scatter.1
  459.1 50.2 all-gather.4
  511.4 49.3 all-gather.2
where the time goes:
time: 596 us; the launch traced here: 590 us
  waiting for transfers between devices  297 us (50%)
  other arithmetic  123 us (21%)
  matrix products  96.2 us (16%)
  blocking collectives  40.1 us (7%)
  between operations  17 us (3%)
  local copies, waits for them, and re-layouts  16.2 us (3%)
    psum x1, waiting for transfers between devices, on_device(): lax.psum(jnp.dot(buffer, right_in, preferred_element_type=jnp.float32), '...  159 us
    another operation x14, other arithmetic, orthonormal(): factor_low = jnp.linalg.cholesky(gram_mat)  78.8 us
    reduce_scatter x1, waiting for transfers between devices, on_device(): lax.psum_scatter(back_part, 'row', scatter_dimension=0, tiled=True)  62.3 us
    psum x1, blocking collectives, on_device(): squares = lax.psum(jnp.sum(back_share * back_share, axis=0), ('row', 'col'))  40.1 us
    another operation x3, other arithmetic, orthonormal(): lax.linalg.triangular_solve(factor_low, left_prod, left_side=False, lower...  39.6 us
    psum x1, waiting for transfers between devices, on_device(): gram_mat = lax.psum(gram_of(left_prod), 'row')  35 us
    all_gather x1, waiting for transfers between devices, on_device(): lax.all_gather(right_share, 'row', axis=0, tiled=True)  31.7 us
    dot_general x1, matrix products, on_device(): jnp.einsum('ik,jk->ij', ortho_rows, back_half, preferred_element_type=jnp...  19.6 us
  transfers between devices with their start and end apart: 5, of which 5 were waited for; matrix products, arithmetic and copies ran while one was open for 4% of the time, Pallas kernels for 0%

commit v1 on v0

v1 whole, which is shorter than its diff:
```python
import jax
import jax.numpy as jnp
from jax import lax
from jax.experimental import pallas as pl
from jax.experimental.pallas import tpu as pltpu
from jax.sharding import PartitionSpec as P

FEEDBACK_CUT = 0.25
STEP_SIZE = 0.1
EPSILON_SQ = 1e-06
PANEL = 32
LANES = 128

f32 = jnp.float32
bf16 = jnp.bfloat16


def split3(value):
    one = value.astype(bf16)
    rest = value - one.astype(f32)
    two = rest.astype(bf16)
    three = (rest - two.astype(f32)).astype(bf16)
    return one, two, three


def inverse_factor_kernel(gram_ref, one_ref, two_ref, work):
    size = gram_ref.shape[0]
    tiles = size // LANES
    work[...] = gram_ref[...]

    @pl.loop(0, size // PANEL)
    def _(panel):
        top = pl.multiple_of(panel * PANEL, PANEL)
        tile = pl.multiple_of((top // LANES) * LANES, LANES)
        rows = work[pl.ds(top, PANEL), :]
        diag = pltpu.roll(
            work[pl.ds(top, PANEL), pl.ds(tile, LANES)], lax.rem(LANES - (top - tile), LANES), 1
        )
        lane = lax.broadcasted_iota(jnp.int32, (PANEL, size), 1)
        row = lax.broadcasted_iota(jnp.int32, (PANEL, size), 0)
        inside = (lane >= top) & (lane < top + PANEL)
        rows = jnp.where(inside, jnp.where(lane - top == row, 1.0, 0.0).astype(f32), rows)
        sub = lax.broadcasted_iota(jnp.int32, (PANEL, LANES), 0)
        cols = [
            jnp.broadcast_to(diag[k // 8 * 8 :, k : k + 1], (PANEL - k // 8 * 8, LANES))
            for k in range(PANEL)
        ]
        pivots = jnp.zeros((PANEL, LANES), f32)
        for j in range(PANEL):
            low = j // 8 * 8
            col = cols[j]
            pivot = col[j - low : j - low + 1, :]
            pivots = jnp.where(sub == j, pivot, pivots)
            if j == PANEL - 1:
                break
            factor = jnp.where(sub[low:] > j, col * (1.0 / pivot), 0.0)
            for k in range(j + 1, PANEL):
                cols[k] = cols[k] - col[k // 8 * 8 - low :, :] * factor[k - low : k - low + 1, :]
            step = jnp.concatenate([factor] * tiles, axis=1) * rows[j : j + 1, :]
            rows = jnp.concatenate([rows[:low], rows[low:] - step], axis=0) if low else rows - step
        scale = lax.rsqrt(pivots)
        scale = scale * (1.5 - 0.5 * pivots * scale * scale)
        rows = rows * jnp.concatenate([scale] * tiles, axis=1)
        work[pl.ds(top, PANEL), :] = rows
        b1, b2, b3 = split3(rows)
        a1, a2, a3 = split3(jnp.where(lane >= top + PANEL, rows, 0.0))
        lhs = jnp.concatenate([a1, a1, a2, a1, a2, a3], axis=0)
        rhs = jnp.concatenate([b1, b2, b1, b3, b2, b1], axis=0)
        for c in range(tiles):
            at = slice(c * LANES, (c + 1) * LANES)

            @pl.when((c + 1) * LANES > top + PANEL)
            def _():
                change = lax.dot_general(
                    lhs[:, at], rhs, (((0,), (0,)), ((), ())), preferred_element_type=f32
                )
                across = lax.broadcasted_iota(jnp.int32, (LANES, size), 1)
                down = lax.broadcasted_iota(jnp.int32, (LANES, size), 0) + c * LANES
                gone = (across >= top) & (across < top + PANEL) & (down >= top + PANEL)
                work[at, :] = jnp.where(gone, 0.0, work[at, :]) - change

    across = lax.broadcasted_iota(jnp.int32, (size, size), 1)
    down = lax.broadcasted_iota(jnp.int32, (size, size), 0)
    inverse = jnp.where(across <= down, work[...], 0.0)
    one = inverse.astype(bf16)
    one_ref[...] = one
    two_ref[...] = (inverse - one.astype(f32)).astype(bf16)


def inverse_factor(gram_mat):
    size = gram_mat.shape[0]
    return pl.pallas_call(
        inverse_factor_kernel,
        out_shape=[jax.ShapeDtypeStruct((size, size), bf16)] * 2,
        in_specs=[pl.BlockSpec(memory_space=pltpu.VMEM)],
        out_specs=[pl.BlockSpec(memory_space=pltpu.VMEM)] * 2,
        scratch_shapes=[pltpu.VMEM((size, size), f32)],
        compiler_params=pltpu.CompilerParams(vmem_limit_bytes=24 << 20),
        cost_estimate=pl.CostEstimate(flops=int(2e10), bytes_accessed=2 << 20, transcendentals=0),
        name="inverse_factor",
    )(gram_mat)


def swap(value, axis, count, bit):
    return lax.ppermute(value, axis, [(i, i ^ bit) for i in range(count)])


def take(value, part, parts):
    share = value.shape[0] // parts
    return lax.dynamic_slice_in_dim(value, part * share, share, 0)


def sum_share(value, axis, count):
    me = lax.axis_index(axis)
    bit = 1
    while bit < count:
        mine = (me // bit) % 2
        got = swap(take(value, 1 - mine, 2).astype(bf16), axis, count, bit)
        value = take(value, mine, 2) + got.astype(f32)
        bit *= 2
    return value


def join_shares(value, axis, count):
    me = lax.axis_index(axis)
    bit = count // 2
    while bit >= 1:
        got = swap(value, axis, count, bit)
        first = (me // bit) % 2 == 0
        value = jnp.concatenate([jnp.where(first, value, got), jnp.where(first, got, value)], axis=0)
        bit //= 2
    return value


def sum_all(value, axis, count, low=1):
    bit = low
    while bit < count:
        value = value + swap(value, axis, count, bit)
        bit *= 2
    return value


def make_on_device(n_row, n_col):
    def on_device(weight, momentum, grad, right_factor):
        full = right_factor.shape[0] * n_col
        core = lax.axis_index("row") % 2
        buffer = (momentum.astype(f32) + grad.astype(f32)).astype(bf16)
        right_in = right_factor.astype(bf16)
        left_part = jnp.dot(buffer, right_in, preferred_element_type=f32)
        left_share = sum_share(left_part, "col", n_col).astype(bf16)
        left_prod = join_shares(left_share, "col", n_col)

        gram_part = lax.dot_general(
            left_prod, left_prod, (((0,), (0,)), ((), ())), preferred_element_type=f32
        )
        gram_half = take(gram_part, core, 2) + swap(take(gram_part, 1 - core, 2), "row", n_row, 1)
        gram_half = sum_all(gram_half, "row", n_row, 2)
        gram_other = swap(gram_half, "row", n_row, 1)
        gram_mat = jnp.concatenate(
            [
                jnp.where(core == 0, gram_half, gram_other),
                jnp.where(core == 0, gram_other, gram_half),
            ],
            axis=0,
        )

        inv_one, inv_two = inverse_factor(gram_mat)
        ortho_rows = (
            lax.dot_general(left_prod, inv_one, (((1,), (1,)), ((), ())), preferred_element_type=f32)
            + lax.dot_general(left_prod, inv_two, (((1,), (1,)), ((), ())), preferred_element_type=f32)
        ).astype(bf16)

        back_part = lax.dot_general(
            buffer, ortho_rows, (((0,), (0,)), ((), ())), preferred_element_type=f32
        )
        sent = take(back_part, 1 - core, 2).astype(bf16)
        back_own = take(back_part, core, 2) + swap(sent, "row", n_row, 1).astype(f32)
        bit = 2
        while bit < n_row:
            sent = back_own.astype(bf16)
            back_own = sent.astype(f32) + swap(sent, "row", n_row, bit).astype(f32)
            bit *= 2
        squares = jnp.sum(back_own * back_own, axis=0, keepdims=True)
        back_own = back_own.astype(bf16)
        back_other = swap(back_own, "row", n_row, 1)
        back_half = jnp.concatenate(
            [
                jnp.where(core == 0, back_own, back_other),
                jnp.where(core == 0, back_other, back_own),
            ],
            axis=0,
        )
        squares = squares + swap(squares, "row", n_row, 1)
        squares = sum_all(squares, "col", n_col)
        scale = jnp.sqrt(f32(full)) / jnp.sqrt(squares + EPSILON_SQ)

        feedback = jnp.einsum("ik,jk->ij", ortho_rows, back_half, preferred_element_type=f32)
        momentum_next = (buffer.astype(f32) - FEEDBACK_CUT * feedback).astype(bf16)
        right_next = back_half.astype(f32) * scale
        right_half = right_next.astype(bf16)
        update = jnp.einsum("ik,jk->ij", ortho_rows, right_half, preferred_element_type=f32)
        weight_next = (weight.astype(f32) - STEP_SIZE * update).astype(bf16)
        return (weight_next, momentum_next, right_next)

    return on_device


def solution(mesh):
    in_specs = (P("row", "col"), P("row", "col"), P("row", "col"), P("col", None))
    out_specs = (P("row", "col"), P("row", "col"), P("col", None))
    return jax.shard_map(
        make_on_device(mesh.shape["row"], mesh.shape["col"]),
        mesh=mesh,
        in_specs=in_specs,
        out_specs=out_specs,
        check_vma=False,
    )
```

time: 596 us -> 285 us (0.48)
  waiting for transfers between devices: 297 us -> 166 us
  other arithmetic: 123 us -> 13.9 us
  blocking collectives: 40.1 us -> 0 us
  matrix products: 96.2 us -> 64.3 us
  Pallas kernels: 0 us -> 20 us
  between operations: 17 us -> 0.96 us
  starting transfers between devices: 0.42 us -> 12.7 us
  local copies, waits for them, and re-layouts: 16.2 us -> 6.19 us
    psum x2 -> x0, waiting for transfers between devices: 194 us -> none  [the longest x1 159 us: on_device(): lax.psum(jnp.dot(buffer, right_in, preferred_element_type=jnp.float32), '...]
    ppermute x0 -> x16, waiting for transfers between devices: none -> 166 us  [swap(): return lax.ppermute(value, axis, [(i, i ^ bit) for i in range(count)])]
    another operation x17 -> x0, other arithmetic: 118 us -> none  [the longest x14 78.8 us: orthonormal(): factor_low = jnp.linalg.cholesky(gram_mat)]
    reduce_scatter x1 -> x0, waiting for transfers between devices: 62.3 us -> none  [on_device(): lax.psum_scatter(back_part, 'row', scatter_dimension=0, tiled=True)]
    all_gather x2 -> x0, waiting for transfers between devices: 40.1 us -> none  [the longest x1 31.7 us: on_device(): lax.all_gather(right_share, 'row', axis=0, tiled=True)]
    psum x1 -> x0, blocking collectives: 40.1 us -> none  [on_device(): squares = lax.psum(jnp.sum(back_share * back_share, axis=0), ('row', 'col'))]
    pallas_call x0 -> x1, Pallas kernels: none -> 20 us  [inverse_factor(): pl.pallas_call(inverse_factor_kernel, out_shape=[jax.ShapeDtypeStruct((si...]
    another operation x13 -> x0, matrix products: 19.8 us -> none  [the longest x7 18 us: orthonormal(): lax.linalg.triangular_solve(factor_low, left_prod, left_side=False, lower...]
  transfers between devices with their start and end apart: 5 -> 16, of which waited for: 5 -> 15; matrix products, arithmetic and copies ran while one was open for 4% -> 0% of each run, Pallas kernels for 0% -> 0%
where the time goes in v1:
time: 285 us; the launch traced here: 284 us
  waiting for transfers between devices  166 us (58%)
  matrix products  64.3 us (23%)
  Pallas kernels  20 us (7%)
  other arithmetic  13.9 us (5%)
  starting transfers between devices  12.7 us (4%)
  local copies, waits for them, and re-layouts  6.19 us (2%)
    ppermute x16, waiting for transfers between devices, swap(): return lax.ppermute(value, axis, [(i, i ^ bit) for i in range(count)])  166 us
    pallas_call x1, Pallas kernels, inverse_factor(): pl.pallas_call(inverse_factor_kernel, out_shape=[jax.ShapeDtypeStruct((si...  20 us
    dot_general x1, matrix products, on_device(): jnp.einsum('ik,jk->ij', ortho_rows, back_half, preferred_element_type=f32)  17.6 us
    dot_general x1, matrix products, on_device(): jnp.einsum('ik,jk->ij', ortho_rows, right_half, preferred_element_type=f32)  15.2 us
    dot_general x1, matrix products, on_device(): left_part = jnp.dot(buffer, right_in, preferred_element_type=f32)  14.4 us
    dot_general x1, matrix products, on_device(): lax.dot_general(buffer, ortho_rows, (((0,), (0,)), ((), ())), preferred_e...  13.3 us
    ppermute x16, starting transfers between devices, swap(): return lax.ppermute(value, axis, [(i, i ^ bit) for i in range(count)])  12.7 us
  transfers between devices with their start and end apart: 16, of which 15 were waited for; matrix products, arithmetic and copies ran while one was open for 0% of the time, Pallas kernels for 0%

profile of v1, /device:TPU:0, one launch (start us, length us, event | category | flops | bytes accessed | tf_op | source)
XLA Modules:
  0.0 284.3 jit_solution(9509148614412777016)
XLA Ops:
  0.7 14.4 %fusion.1 = f32[2048,512]{1,0:T(8,128)S(1)} fusion(f32[3328,512]{1,0:T(8,128)} %param.7, bf16[2048,3328]{1,0:T(8,128)(2,1)} %param.6, bf16[2048,3328]{1,0:T(8,128)(2,1)} %param.5), kind=kOutput, calls=%fused_computation.11 | convolution fusion | flops 7008288768 | bytes 38273024 | tf_op jit(solution)/shard_map/dot_general | solution.py:149
  17.2 3.0 %collective-permute-start = (bf16[1024,512]{1,0:T(8,128)(2,1)S(1)}, bf16[1024,512]{1,0:T(8,128)(2,1)S(1)}, u32[]{:S(2)}, u32[]{:S(2)}) collective-permute-start(bf16[1024,512]{1,0:T(8,128)(2,1)S(1)} %dynamic-slice_convert_fusion.1), channel_id=1, source_target_pairs={{0,1},{1,0},{2,3},{3,2},{4,5},{5,4},{6,7},{7,6},{8,9},{9,8},{10,11... | collective-permute-start | bytes 3145736 | tf_op jit(solution)/shard_map/ppermute | solution.py:105
  20.2 23.2 %collective-permute-done = bf16[1024,512]{1,0:T(8,128)(2,1)S(1)} collective-permute-done((bf16[1024,512]{1,0:T(8,128)(2,1)S(1)}, bf16[1024,512]{1,0:T(8,128)(2,1)S(1)}, u32[]{:S(2)}, u32[]{:S(2)}) %collective-permute-start) | collective-permute-done | bytes 1048608 | tf_op jit(solution)/shard_map/ppermute | solution.py:105
  47.3 11.4 %collective-permute-done.1 = bf16[512,512]{1,0:T(8,128)(2,1)} collective-permute-done((bf16[512,512]{1,0:T(8,128)(2,1)S(1)}, bf16[512,512]{1,0:T(8,128)(2,1)}, u32[]{:S(2)}, u32[]{:S(2)}) %collective-permute-start.1) | collective-permute-done | bytes 524320 | tf_op jit(solution)/shard_map/ppermute | solution.py:105
  59.9 2.6 collective-permute-start.2
  62.5 10.6 %collective-permute-done.2 = bf16[256,512]{1,0:T(8,128)(2,1)S(1)} collective-permute-done((bf16[256,512]{1,0:T(8,128)(2,1)S(1)}, bf16[256,512]{1,0:T(8,128)(2,1)S(1)}, u32[]{:S(2)}, u32[]{:S(2)}) %collective-permute-start.2) | collective-permute-done | bytes 262176 | tf_op jit(solution)/shard_map/ppermute | solution.py:105
  73.2 14.0 %collective-permute-done.3 = bf16[256,512]{1,0:T(8,128)(2,1)S(1)} collective-permute-done((bf16[256,512]{1,0:T(8,128)(2,1)S(1)}, bf16[256,512]{1,0:T(8,128)(2,1)S(1)}, u32[]{:S(2)}, u32[]{:S(2)}) %collective-permute-start.3) | collective-permute-done | bytes 262176 | tf_op jit(solution)/shard_map/ppermute | solution.py:105
  87.4 12.6 %collective-permute-done.4 = bf16[512,512]{1,0:T(8,128)(2,1)S(1)} collective-permute-done((bf16[512,512]{1,0:T(8,128)(2,1)S(1)}, bf16[512,512]{1,0:T(8,128)(2,1)S(1)}, u32[]{:S(2)}, u32[]{:S(2)}) %collective-permute-start.4) | collective-permute-done | bytes 524320 | tf_op jit(solution)/shard_map/ppermute | solution.py:105
  100.4 23.0 %collective-permute-done.5 = bf16[1024,512]{1,0:T(8,128)(2,1)} collective-permute-done((bf16[1024,512]{1,0:T(8,128)(2,1)S(1)}, bf16[1024,512]{1,0:T(8,128)(2,1)}, u32[]{:S(2)}, u32[]{:S(2)}) %collective-permute-start.5) | collective-permute-done | bytes 1048608 | tf_op jit(solution)/shard_map/ppermute | solution.py:105
  127.1 2.2 collective-permute-done.6
  130.6 14.0 %collective-permute-done.7 = f32[256,512]{1,0:T(8,128)S(1)} collective-permute-done((f32[256,512]{1,0:T(8,128)S(1)}, f32[256,512]{1,0:T(8,128)S(1)}, u32[]{:S(2)}, u32[]{:S(2)}) %collective-permute-start.7) | collective-permute-done | bytes 524320 | tf_op jit(solution)/shard_map/ppermute | solution.py:105
  146.8 20.0 %inverse_factor.1 = (bf16[512,512]{1,0:T(8,128)(2,1)S(1)}, bf16[512,512]{1,0:T(8,128)(2,1)S(1)}) custom-call(f32[512,512]{1,0:T(8,128)S(1)} %pad_maximum_fusion.4.gram_ref), custom_call_target="tpu_custom_call" | custom-call | flops 20000000000 | bytes 2097152 | tf_op jit(solution)/shard_map/inverse_factor/pallas_call | solution.py:92
  169.4 13.3 %fusion.10 = f32[3328,512]{1,0:T(8,128)S(1)} fusion(bf16[2048,512]{1,0:T(8,128)(2,1)S(1)} %add_convert_fusion.1, bf16[2048,3328]{1,0:T(8,128)(2,1)} %param.6, bf16[2048,3328]{1,0:T(8,128)(2,1)} %param.5), kind=kOutput, calls=%fused_computation.43 | convolution fusion | flops 7006584832 | bytes 36175872 | tf_op jit(solution)/shard_map/dot_general | solution.py:173
  182.7 2.9 %copy-done = f32[3328,512]{1,0:T(8,128)} copy-done((f32[3328,512]{1,0:T(8,128)}, f32[3328,512]{1,0:T(8,128)S(1)}, u32[]{:S(2)}) %copy-start) | copy-done | bytes 6815768
  186.0 3.5 %collective-permute-done.9 = bf16[1664,512]{1,0:T(8,128)(2,1)S(1)} collective-permute-done((bf16[1664,512]{1,0:T(8,128)(2,1)S(1)}, bf16[1664,512]{1,0:T(8,128)(2,1)S(1)}, u32[]{:S(2)}, u32[]{:S(2)}) %collective-permute-start.9) | collective-permute-done | bytes 1703968 | tf_op jit(solution)/shard_map/ppermute | solution.py:105
  189.4 2.5 add_convert_fusion.2
  192.3 39.0 %collective-permute-done.10 = bf16[1664,512]{1,0:T(8,128)(2,1)S(1)} collective-permute-done((bf16[1664,512]{1,0:T(8,128)(2,1)S(1)}, bf16[1664,512]{1,0:T(8,128)(2,1)S(1)}, u32[]{:S(2)}, u32[]{:S(2)}) %collective-permute-start.10) | collective-permute-done | bytes 1703968 | tf_op jit(solution)/shard_map/ppermute | solution.py:105
  232.6 3.1 %collective-permute-done.12 = f32[1,512]{1,0:T(1,128)S(1)} collective-permute-done((f32[1,512]{1,0:T(1,128)S(1)}, f32[1,512]{1,0:T(1,128)S(1)}, u32[]{:S(2)}, u32[]{:S(2)}) %collective-permute-start.12) | collective-permute-done | bytes 2080 | tf_op jit(solution)/shard_map/ppermute | solution.py:105
  236.0 3.3 %collective-permute-done.13 = f32[1,512]{1,0:T(1,128)S(1)} collective-permute-done((f32[1,512]{1,0:T(1,128)S(1)}, f32[1,512]{1,0:T(1,128)S(1)}, u32[]{:S(2)}, u32[]{:S(2)}) %collective-permute-start.13) | collective-permute-done | bytes 2080 | tf_op jit(solution)/shard_map/ppermute | solution.py:105
  239.8 3.0 %collective-permute-done.14 = f32[1,512]{1,0:T(1,128)S(1)} collective-permute-done((f32[1,512]{1,0:T(1,128)S(1)}, f32[1,512]{1,0:T(1,128)S(1)}, u32[]{:S(2)}, u32[]{:S(2)}) %collective-permute-start.14) | collective-permute-done | bytes 2080 | tf_op jit(solution)/shard_map/ppermute | solution.py:105
  242.9 2.9 %collective-permute-start.15 = (f32[1,512]{1,0:T(1,128)S(1)}, f32[1,512]{1,0:T(1,128)S(1)}, u32[]{:S(2)}, u32[]{:S(2)}) collective-permute-start(f32[1,512]{1,0:T(1,128)S(1)} %add.119), channel_id=1, source_target_pairs={{0,4},{1,5},{2,6},{3,7},{4,0},{5,1},{6,2},{7,3},{8,12},{9,13},{10,... | collective-permute-start | bytes 6152 | tf_op jit(solution)/shard_map/ppermute | solution.py:105
  247.6 17.6 %subtract_convert_fusion = bf16[2048,3328]{1,0:T(8,128)(2,1)} fusion(bf16[2048,512]{1,0:T(8,128)(2,1)S(1)} %copy-done.3, bf16[1664,512]{1,0:T(8,128)(2,1)S(1)} %get-tuple-element.8, bf16[1664,512]{1,0:T(8,128)(2,1)S(1)} %get-tuple-element.7, bf16[2048,3328]{1,0:T(8,128)(2,1)} %param.6, bf16[2048,3328]{1,0:T(8,128)(2,1)} %param.5), kind=kOutput, calls=%fused_computation | convolution fusion | flops 7040663552 | bytes 46399488 | tf_op jit(solution)/shard_map/ik,jk->ij/dot_general | solution.py:197
  265.2 3.9 %convert_multiply_fusion = f32[3328,512]{1,0:T(8,128)} fusion(f32[512]{0:T(512)S(1)} %bitcast.9, bf16[1664,512]{1,0:T(8,128)(2,1)S(1)} %get-tuple-element.8, bf16[1664,512]{1,0:T(8,128)(2,1)S(1)} %get-tuple-element.7), kind=kLoop, calls=%fused_computation.3 | loop fusion | flops 8519680 | bytes 10225664 | tf_op jit(solution)/shard_map/mul | solution.py:199
  269.0 15.2 %subtract_convert_fusion.1 = bf16[2048,3328]{1,0:T(8,128)(2,1)} fusion(bf16[2048,3328]{1,0:T(8,128)(2,1)} %param.4, bf16[2048,512]{1,0:T(8,128)(2,1)S(1)} %copy-done.3, f32[3328,512]{1,0:T(8,128)} %convert_multiply_fusion), kind=kOutput, calls=%fused_computation.1 | convolution fusion | flops 7008288768 | bytes 36175872 | tf_op jit(solution)/shard_map/ik,jk->ij/dot_general | solution.py:201
  (49 shorter events, 22.4 us)
Async XLA Ops:
  15.1 2.0 copy-start.1
  17.2 26.2 %collective-permute-start = (bf16[1024,512]{1,0:T(8,128)(2,1)S(1)}, bf16[1024,512]{1,0:T(8,128)(2,1)S(1)}, u32[]{:S(2)}, u32[]{:S(2)}) collective-permute-start(bf16[1024,512]{1,0:T(8,128)(2,1)S(1)} %dynamic-slice_convert_fusion.1), channel_id=1, source_target_pairs={{0,1},{1,0},{2,3},{3,2},{4,5},{5,4},{6,7},{7,6},{8,9},{9,8},{10,11... | collective-permute-start | bytes 3145736 | tf_op jit(solution)/shard_map/ppermute | solution.py:105
  45.4 13.3 %collective-permute-start.1 = (bf16[512,512]{1,0:T(8,128)(2,1)S(1)}, bf16[512,512]{1,0:T(8,128)(2,1)}, u32[]{:S(2)}, u32[]{:S(2)}) collective-permute-start(bf16[512,512]{1,0:T(8,128)(2,1)S(1)} %dynamic-slice_convert_fusion.2), channel_id=1, source_target_pairs={{0,2},{1,3},{2,0},{3,1},{4,6},{5,7},{6,4},{7,5},{8,10},{9,11},{10,... | collective-permute-start | bytes 1572872 | tf_op jit(solution)/shard_map/ppermute | solution.py:105
  59.9 13.1 %collective-permute-start.2 = (bf16[256,512]{1,0:T(8,128)(2,1)S(1)}, bf16[256,512]{1,0:T(8,128)(2,1)S(1)}, u32[]{:S(2)}, u32[]{:S(2)}) collective-permute-start(bf16[256,512]{1,0:T(8,128)(2,1)S(1)} %dynamic-slice_convert_fusion.3), channel_id=1, source_target_pairs={{0,4},{1,5},{2,6},{3,7},{4,0},{5,1},{6,2},{7,3},{8,12},{9,13},{10,... | collective-permute-start | bytes 786440 | tf_op jit(solution)/shard_map/ppermute | solution.py:105
  73.1 14.1 %collective-permute-start.3 = (bf16[256,512]{1,0:T(8,128)(2,1)S(1)}, bf16[256,512]{1,0:T(8,128)(2,1)S(1)}, u32[]{:S(2)}, u32[]{:S(2)}) collective-permute-start(bf16[256,512]{1,0:T(8,128)(2,1)S(1)} %add_convert_fusion.3), channel_id=1, source_target_pairs={{0,4},{1,5},{2,6},{3,7},{4,0},{5,1},{6,2},{7,3},{8,12},{9,13},{10,... | collective-permute-start | bytes 786440 | tf_op jit(solution)/shard_map/ppermute | solution.py:105
  87.3 12.7 %collective-permute-start.4 = (bf16[512,512]{1,0:T(8,128)(2,1)S(1)}, bf16[512,512]{1,0:T(8,128)(2,1)S(1)}, u32[]{:S(2)}, u32[]{:S(2)}) collective-permute-start(bf16[512,512]{1,0:T(8,128)(2,1)S(1)} %pad_maximum_fusion.8), channel_id=1, source_target_pairs={{0,2},{1,3},{2,0},{3,1},{4,6},{5,7},{6,4},{7,5},{8,10},{9,11},{10,... | collective-permute-start | bytes 1572872 | tf_op jit(solution)/shard_map/ppermute | solution.py:105
  100.3 23.1 %collective-permute-start.5 = (bf16[1024,512]{1,0:T(8,128)(2,1)S(1)}, bf16[1024,512]{1,0:T(8,128)(2,1)}, u32[]{:S(2)}, u32[]{:S(2)}) collective-permute-start(bf16[1024,512]{1,0:T(8,128)(2,1)S(1)} %pad_maximum_fusion.3), channel_id=1, source_target_pairs={{0,1},{1,0},{2,3},{3,2},{4,5},{5,4},{6,7},{7,6},{8,9},{9,8},{10,11... | collective-permute-start | bytes 3145736 | tf_op jit(solution)/shard_map/ppermute | solution.py:105
  127.1 2.3 collective-permute-start.6
  130.5 14.0 %collective-permute-start.7 = (f32[256,512]{1,0:T(8,128)S(1)}, f32[256,512]{1,0:T(8,128)S(1)}, u32[]{:S(2)}, u32[]{:S(2)}) collective-permute-start(f32[256,512]{1,0:T(8,128)S(1)} %dynamic-slice_add_fusion), channel_id=1, source_target_pairs={{0,16},{8,24},{16,0},{24,8},{1,17},{9,25},{17,1},{25,9},{2,18},{10... | collective-permute-start | bytes 1572872 | tf_op jit(solution)/shard_map/ppermute | solution.py:105
  144.6 2.0 collective-permute-start.8
  169.4 13.3 %copy-start.2 = (bf16[2048,512]{1,0:T(8,128)(2,1)}, bf16[2048,512]{1,0:T(8,128)(2,1)S(1)}, u32[]{:S(2)}) copy-start(bf16[2048,512]{1,0:T(8,128)(2,1)S(1)} %add_convert_fusion.1) | copy-start | bytes 6291460
  182.7 2.9 %copy-start = (f32[3328,512]{1,0:T(8,128)}, f32[3328,512]{1,0:T(8,128)S(1)}, u32[]{:S(2)}) copy-start(f32[3328,512]{1,0:T(8,128)S(1)} %fusion.10) | copy-start | bytes 20447236
  185.8 3.7 %collective-permute-start.9 = (bf16[1664,512]{1,0:T(8,128)(2,1)S(1)}, bf16[1664,512]{1,0:T(8,128)(2,1)S(1)}, u32[]{:S(2)}, u32[]{:S(2)}) collective-permute-start(bf16[1664,512]{1,0:T(8,128)(2,1)S(1)} %dynamic-slice_convert_fusion), channel_id=1, source_target_pairs={{0,8},{8,0},{16,24},{24,16},{1,9},{9,1},{17,25},{25,17},{2,10},{10... | collective-permute-start | bytes 5111816 | tf_op jit(solution)/shard_map/ppermute | solution.py:105
  192.0 39.3 %collective-permute-start.10 = (bf16[1664,512]{1,0:T(8,128)(2,1)S(1)}, bf16[1664,512]{1,0:T(8,128)(2,1)S(1)}, u32[]{:S(2)}, u32[]{:S(2)}) collective-permute-start(bf16[1664,512]{1,0:T(8,128)(2,1)S(1)} %add_convert_fusion.2), channel_id=1, source_target_pairs={{0,16},{8,24},{16,0},{24,8},{1,17},{9,25},{17,1},{25,9},{2,18},{10... | collective-permute-start | bytes 5111816 | tf_op jit(solution)/shard_map/ppermute | solution.py:105
  232.0 15.6 %copy-start.3 = (bf16[2048,512]{1,0:T(8,128)(2,1)S(1)}, bf16[2048,512]{1,0:T(8,128)(2,1)}, u32[]{:S(2)}) copy-start(bf16[2048,512]{1,0:T(8,128)(2,1)} %copy-done.2) | copy-start | bytes 6291460
  232.0 15.3 %collective-permute-start.11 = (bf16[1664,512]{1,0:T(8,128)(2,1)S(1)}, bf16[1664,512]{1,0:T(8,128)(2,1)S(1)}, u32[]{:S(2)}, u32[]{:S(2)}) collective-permute-start(bf16[1664,512]{1,0:T(8,128)(2,1)S(1)} %get-tuple-element.9), channel_id=1, source_target_pairs={{0,8},{8,0},{16,24},{24,16},{1,9},{9,1},{17,25},{25,17},{2,10},{10... | collective-permute-start | bytes 5111816 | tf_op jit(solution)/shard_map/ppermute | solution.py:105
  232.1 3.6 %collective-permute-start.12 = (f32[1,512]{1,0:T(1,128)S(1)}, f32[1,512]{1,0:T(1,128)S(1)}, u32[]{:S(2)}, u32[]{:S(2)}) collective-permute-start(f32[1,512]{1,0:T(1,128)S(1)} %bitcast.7), channel_id=1, source_target_pairs={{0,8},{8,0},{16,24},{24,16},{1,9},{9,1},{17,25},{25,17},{2,10},{10... | collective-permute-start | bytes 6152 | tf_op jit(solution)/shard_map/ppermute | solution.py:105
  235.7 3.6 %collective-permute-start.13 = (f32[1,512]{1,0:T(1,128)S(1)}, f32[1,512]{1,0:T(1,128)S(1)}, u32[]{:S(2)}, u32[]{:S(2)}) collective-permute-start(f32[1,512]{1,0:T(1,128)S(1)} %add.117), channel_id=1, source_target_pairs={{0,1},{1,0},{2,3},{3,2},{4,5},{5,4},{6,7},{7,6},{8,9},{9,8},{10,11... | collective-permute-start | bytes 6152 | tf_op jit(solution)/shard_map/ppermute | solution.py:105
  239.3 3.6 %collective-permute-start.14 = (f32[1,512]{1,0:T(1,128)S(1)}, f32[1,512]{1,0:T(1,128)S(1)}, u32[]{:S(2)}, u32[]{:S(2)}) collective-permute-start(f32[1,512]{1,0:T(1,128)S(1)} %add.118), channel_id=1, source_target_pairs={{0,2},{1,3},{2,0},{3,1},{4,6},{5,7},{6,4},{7,5},{8,10},{9,11},{10,... | collective-permute-start | bytes 6152 | tf_op jit(solution)/shard_map/ppermute | solution.py:105
  242.9 4.5 %collective-permute-start.15 = (f32[1,512]{1,0:T(1,128)S(1)}, f32[1,512]{1,0:T(1,128)S(1)}, u32[]{:S(2)}, u32[]{:S(2)}) collective-permute-start(f32[1,512]{1,0:T(1,128)S(1)} %add.119), channel_id=1, source_target_pairs={{0,4},{1,5},{2,6},{3,7},{4,0},{5,1},{6,2},{7,3},{8,12},{9,13},{10,... | collective-permute-start | bytes 6152 | tf_op jit(solution)/shard_map/ppermute | solution.py:105
